TPU v7x, 256 devices: a whole 4x4x8 slice. The times are simulated.
256 devices in a mesh: dp: 16 (over z_hi, x, core), slot: 4 (over y), hid: 4 (over z_lo).
Axes of the slice: x: 4, y: 4, z: 8 (z_hi: 2, z_lo: 4; z = z_hi * 4 + z_lo), core: 2. Of those that a mesh axis runs over, the one named last changes fastest.
Arguments:
- master_weights: float32 [8, 3, 768, 2048], P('slot', None, 'hid', 'dp'), may hold values from -0.125 to 0.125
- first_moment: float32 [8, 3, 768, 2048], P('slot', None, 'hid', 'dp'), may hold values from -6 to 6
- second_moment: float32 [8, 3, 768, 2048], P('slot', None, 'hid', 'dp'), may hold values from 1 to 100
- tokens_one: bfloat16 [16384, 2048], P('dp'), may hold values from -6 to 6
- grad_out: bfloat16 [16384, 2048], P('dp'), may hold values from -6 to 6
- route_one: int32 [16384, 2], P('dp'), may hold values from 0 to 7, all different within a row
- prob_one: float32 [16384, 2], P('dp'), may hold values from 0.05 to 0.6
- tokens_two: bfloat16 [16384, 2048], P('dp'), may hold values from -6 to 6
- route_two: int32 [16384, 2], P('dp'), may hold values from 0 to 7, all different within a row
- prob_two: float32 [16384, 2], P('dp'), may hold values from 0.05 to 0.6
- old_order: int32 [8], replicated, may hold values from 0 to 7, each once
- new_order: int32 [8], replicated, may hold values from 0 to 7, each once
Outputs:
- moved_master: float32 [8, 3, 768, 2048], P('slot', None, 'hid', 'dp')
- moved_first: float32 [8, 3, 768, 2048], P('slot', None, 'hid', 'dp')
- moved_second: float32 [8, 3, 768, 2048], P('slot', None, 'hid', 'dp')
- next_output: bfloat16 [16384, 2048], P('dp', ('slot', 'hid'))
Inputs may be any that keep to these rules, and one draw needn't show every extreme that they name: `old_order`: lists each of the 8 experts once. `new_order`: lists each of the 8 experts once. `route_one`: each row names 2 different experts. `route_two`: each row names 2 different experts.
All inputs are finite; a program needn't handle non-finite values.
Results may differ from a plain program's by a relative error of at most 0.017.
Values may be sent and summed in bfloat16 or wider, within the bound.
No kernel may reach another device: no remote copies, remote signals or barrier semaphores. Data moves between devices by JAX's collectives and lax.ppermute only.
A program may use at most 128 MiB of HBM per device.

v0:
```python
import jax
import jax.numpy as jnp
from jax import lax
from jax.sharding import Mesh
from jax.sharding import PartitionSpec as P

DP = ("dp_0", "dp_1", "dp_2")
learn_rate = 0.001
beta_one = 0.9
beta_two = 0.95
epsilon = 1e-08
decay_rate = 0.1


def in_blocks(x, dim, size):
    before, after = (x.shape[:dim], x.shape[dim + 1 :])
    return jnp.moveaxis(x.reshape(*before, size, -1, *after), dim, 0)


def summed_rows(x, chips, core, dim):
    sizes = (lax.axis_size(chips), lax.axis_size(core))
    pieces = in_blocks(x, dim, sizes[0] * sizes[1])
    inside = pieces.shape[1:]
    pieces = pieces.reshape(*sizes, *inside).swapaxes(0, 1).reshape(-1, *inside)
    pieces = lax.psum_scatter(pieces, core, scatter_dimension=0, tiled=True)
    return lax.psum_scatter(pieces, chips, scatter_dimension=0, tiled=True)[0]


def scatter_axes(x, axes, dim):
    if not axes:
        return x
    nearer = lax.psum_scatter(x, axes[0], scatter_dimension=dim, tiled=True)
    return scatter_axes(nearer, axes[1:], dim)


def rows_by(left, right):
    return lax.dot_general(
        left, right, (((1,), (1,)), ((), ())), preferred_element_type=jnp.float32
    )


def cols_by(left, right):
    return lax.dot_general(
        left, right, (((0,), (0,)), ((), ())), preferred_element_type=jnp.float32
    )


def expert_parts(tokens, grad_out, scaling, weights):
    gate_proj = rows_by(tokens, weights[0])
    up_proj = rows_by(tokens, weights[1])
    logistic = jax.nn.sigmoid(gate_proj)
    swish_gate = gate_proj * logistic
    activated = (swish_gate * up_proj).astype(jnp.bfloat16)
    scaled_grad = (scaling[:, None] * grad_out.astype(jnp.float32)).astype(jnp.bfloat16)
    d_activated = rows_by(scaled_grad, weights[2])
    d_gate = (d_activated * up_proj * logistic * (1.0 + gate_proj * (1.0 - logistic))).astype(
        jnp.bfloat16
    )
    d_up = (d_activated * swish_gate).astype(jnp.bfloat16)
    return (d_gate, d_up, activated, scaled_grad)


def expert_out(tokens, scaling, weights):
    gate_proj = rows_by(tokens, weights[0])
    up_proj = rows_by(tokens, weights[1])
    mixed = (scaling[:, None] * gate_proj * jax.nn.sigmoid(gate_proj) * up_proj).astype(
        jnp.bfloat16
    )
    return jnp.dot(mixed, weights[2], preferred_element_type=jnp.float32)


def adamw_update(master, moment_a, moment_b, grad_sum):
    new_a = beta_one * moment_a + (1.0 - beta_one) * grad_sum
    new_b = beta_two * moment_b + (1.0 - beta_two) * grad_sum * grad_sum
    fixed_a = new_a / (1.0 - beta_one**10)
    fixed_b = new_b / (1.0 - beta_two**10)
    new_master = master - learn_rate * (
        fixed_a / (jnp.sqrt(fixed_b) + epsilon) + decay_rate * master
    )
    return (new_master, new_a, new_b)


def coefficients(routes, probs, expert_ids):
    matches = routes[:, :, None] == expert_ids[None, None, :]
    return jnp.sum(jnp.where(matches, probs[:, :, None], 0.0), axis=1)


def per_device(
    master_weights,
    first_moment,
    second_moment,
    tokens_one,
    grad_out,
    route_one,
    prob_one,
    tokens_two,
    route_two,
    prob_two,
    old_order,
    new_order,
):
    local_count = master_weights.shape[0]
    slot_index = lax.axis_index("slot")
    slot_count = lax.axis_size("slot")
    offset = slot_index * local_count
    held_ids = lax.dynamic_slice_in_dim(old_order, offset, local_count)
    shard_weights = master_weights.astype(jnp.bfloat16)
    full_weights = lax.all_gather(shard_weights, DP, axis=3, tiled=True)
    scaling_one = coefficients(route_one, prob_one, held_ids)
    parts = [
        expert_parts(tokens_one, grad_out, scaling_one[:, expert], full_weights[expert])
        for expert in range(local_count)
    ]
    gradients = jnp.stack(
        [
            jnp.stack(
                [
                    cols_by(part[0], tokens_one),
                    cols_by(part[1], tokens_one),
                    cols_by(part[2], part[3]),
                ]
            )
            for part in parts
        ]
    )
    owned_grads = summed_rows(gradients.astype(jnp.bfloat16), ("dp_0", "dp_1"), "dp_2", 3).astype(
        jnp.float32
    )
    new_master, new_a, new_b = adamw_update(
        master_weights, first_moment, second_moment, owned_grads
    )
    positions = jnp.arange(old_order.shape[0], dtype=jnp.int32)
    source = jnp.sum(
        jnp.where(old_order[None, :] == new_order[:, None], positions[None, :], 0), axis=1
    )
    owner_slot = source // local_count
    within = source % local_count
    my_owners = lax.dynamic_slice_in_dim(owner_slot, offset, local_count)
    pick_rows = my_owners * local_count + jnp.arange(local_count, dtype=jnp.int32)

    def outgoing(state_block):
        picked = jnp.take(state_block, within, axis=0)
        return picked.reshape((slot_count, local_count) + state_block.shape[1:])

    arrived = (
        lax.all_to_all(outgoing(new_master), "slot", split_axis=0, concat_axis=0, tiled=True),
        lax.all_to_all(outgoing(new_a), "slot", split_axis=0, concat_axis=0, tiled=True),
        lax.all_to_all(outgoing(new_b), "slot", split_axis=0, concat_axis=0, tiled=True),
    )
    moved_states = tuple(
        (
            jnp.take(
                state_block.reshape((slot_count * local_count,) + state_block.shape[2:]),
                pick_rows,
                axis=0,
            )
            for state_block in arrived
        )
    )
    moved_master, moved_first, moved_second = moved_states
    next_shard = new_master.astype(jnp.bfloat16)
    next_full = lax.all_gather(next_shard, DP, axis=3, tiled=True)
    scaling_two = coefficients(route_two, prob_two, held_ids)
    partial_value = expert_out(tokens_two, scaling_two[:, 0], next_full[0])
    expert = 1
    partial_value = partial_value + expert_out(
        tokens_two, scaling_two[:, expert], next_full[expert]
    )
    mixed_out = scatter_axes(partial_value, ("slot", "hid"), 1).astype(jnp.bfloat16)
    return (moved_master, moved_first, moved_second, mixed_out)


def solution(mesh):
    split = Mesh(
        mesh.devices.reshape(2, 4, 2, mesh.shape["slot"], mesh.shape["hid"]),
        ("dp_0", "dp_1", "dp_2", "slot", "hid"),
    )
    in_specs = (
        P("slot", None, "hid", DP),
        P("slot", None, "hid", DP),
        P("slot", None, "hid", DP),
        P(DP, None),
        P(DP, None),
        P(DP, None),
        P(DP, None),
        P(DP, None),
        P(DP, None),
        P(DP, None),
        P(),
        P(),
    )
    out_specs = (
        P("slot", None, "hid", DP),
        P("slot", None, "hid", DP),
        P("slot", None, "hid", DP),
        P(DP, ("slot", "hid")),
    )
    return jax.shard_map(
        per_device, mesh=split, in_specs=in_specs, out_specs=out_specs, check_vma=False
    )
```

profile of v0, /device:TPU:2, one launch (start us, length us, event | category | flops | bytes accessed | tf_op | source)
XLA Modules:
  0.0 531.8 jit_solution(10620187443816465604)
XLA Ops:
  10.7 85.3 %all-gather.3.cloned.1.call-done = bf16[2,3,192,2048]{3,2,1,0:T(8,128)(2,1)} async-done(((bf16[2,3,192,128]{3,2,1,0:T(8,128)(2,1)}), bf16[2,3,192,2048]{3,2,1,0:T(8,128)(2,1)}) %all-gather.3.cloned.1.call-update) | async-done | bytes 4718608 | tf_op jit(solution)/shard_map/all_gather | solution.py:108
  96.0 4.1 fusion.24
  100.1 3.9 fusion.23
  119.9 3.4 copy.26
  123.3 14.0 %reduce-scatter.5.cloned.1.call-done = bf16[8,2,3,192,128]{4,3,2,1,0:T(8,128)(2,1)} async-done(((bf16[16,2,3,192,128]{4,3,2,1,0:T(8,128)(2,1)}), bf16[8,2,3,192,128]{4,3,2,1,0:T(8,128)(2,1)}) %reduce-scatter.5.cloned.1.call-update) | async-done | bytes 2359312 | tf_op jit(solution)/shard_map/reduce_scatter | solution.py:25
  137.4 105.3 %reduce-scatter.7.cloned.1.call-done = bf16[1,2,3,192,128]{4,3,2,1,0:T(8,128)(2,1)} async-done(((bf16[8,2,3,192,128]{4,3,2,1,0:T(8,128)(2,1)}), bf16[1,2,3,192,128]{4,3,2,1,0:T(8,128)(2,1)}) %reduce-scatter.7.cloned.1.call-update) | async-done | bytes 294928 | tf_op jit(solution)/shard_map/reduce_scatter | solution.py:26
  242.7 2.2 fusion.63
  244.9 78.6 %all-gather.5.cloned.1.call-done = bf16[2,3,192,2048]{3,2,1,0:T(8,128)(2,1)} async-done(((bf16[2,3,192,128]{3,2,1,0:T(8,128)(2,1)}), bf16[2,3,192,2048]{3,2,1,0:T(8,128)(2,1)}) %all-gather.5.cloned.1.call-update) | async-done | bytes 4718608 | tf_op jit(solution)/shard_map/all_gather | solution.py:162
  323.5 4.1 fusion.22
  327.7 2.7 fusion.21
  330.3 8.6 %fusion.19 = f32[1024,2048]{1,0:T(8,128)} fusion(bf16[1024,2048]{1,0:T(8,128)(2,1)} %param.23, bf16[2,3,192,2048]{3,2,1,0:T(8,128)(2,1)} %all-gather.5.cloned.1.call-done, f32[192,1024]{1,0:T(8,128)S(1)} %fusion.22, f32[1024]{0:T(1024)S(1)} %bitcast.109), kind=kOutput, calls=%fused_computation.29 | convolution fusion | flops 1611988992 | bytes 14946304 | tf_op jit(solution)/shard_map/dot_general | solution.py:69
  338.9 11.1 %convolution_add_fusion = f32[1024,2048]{1,0:T(8,128)} fusion(f32[1024,2048]{1,0:T(8,128)} %fusion.19, bf16[1024,2048]{1,0:T(8,128)(2,1)} %param.23, bf16[2,3,192,2048]{3,2,1,0:T(8,128)(2,1)} %all-gather.5.cloned.1.call-done, f32[192,1024]{1,0:T(8,128)S(1)} %fusion.21, f32[1024]{0:T(1024)S(1)} %bitcast.108), kind=kOutput, calls=%fused_computation.11 | convolution fusion | flops 1614086144 | bytes 23334912 | tf_op jit(solution)/shard_map/dot_general | solution.py:69
  350.9 2.1 gather_fusion.4
  353.0 2.2 gather_fusion.2
  355.2 2.2 gather_fusion
  357.3 6.7 %broadcast_select_fusion = (f32[8,3,192,128]{3,2,1,0:T(8,128)}, f32[8,3,192,128]{3,2,1,0:T(8,128)S(1)}, f32[8,3,192,128]{3,2,1,0:T(8,128)}) fusion(f32[8,3,192,128]{3,2,1,0:T(8,128)} %gather_fusion.4, pred[8]{0:T(512)(128)(4,1)S(1)} %get-tuple-element.14, f32[8,3,192,128]{3,2,1,0:T(8,128)} %gather_fusion.2, f32[8,3,192,128]{3,2,1,0:T(8,128)} %gather_fusion), kind=kLoop, calls=%fused_computation.31 | loop fusion | flops 1769472 | bytes 14155784 | tf_op jit(solution)/shard_map/jit(_take)/select_n | solution.py:142
  364.0 4.5 all-to-all-start.2
  368.6 85.9 %reduce-scatter.9.cloned.1.call-done = f32[1024,512]{1,0:T(8,128)} async-done(((f32[1024,2048]{1,0:T(8,128)}), f32[1024,512]{1,0:T(8,128)}) %reduce-scatter.9.cloned.1.call-update) | async-done | bytes 2097168 | tf_op jit(solution)/shard_map/reduce_scatter | solution.py:32
  454.6 32.7 %all_to_all.15 = f32[4,2,3,192,128]{4,3,2,1,0:T(8,128)} all-to-all(f32[4,2,3,192,128]{4,3,2,1,0:T(8,128)S(1)} %bitcast.98), channel_id=1, replica_groups=mesh['dp_0'=2,'dp_1'=4,'dp_2'=2,'slot'=4,'hid'=4] {'slot'}, dimensions={0} | all-to-all | bytes 4718592 | tf_op jit(solution)/shard_map/all_to_all | solution.py:147
  487.3 3.6 all-to-all-start
  491.1 2.2 gather_fusion.5
  493.3 2.2 gather_fusion.3
  495.6 23.8 %all-to-all-done = f32[4,2,3,192,128]{4,3,2,1,0:T(8,128)S(1)} async-done(((f32[4,2,3,192,128]{4,3,2,1,0:T(8,128)}), f32[4,2,3,192,128]{4,3,2,1,0:T(8,128)S(1)}, u32[]{:S(2)}, u32[]{:S(2)}) %all-to-all-start) | async-done | bytes 2359328 | tf_op jit(solution)/shard_map/all_to_all | solution.py:146
  520.8 2.4 broadcast_select_fusion.3
  (61 shorter events, 23.6 us)
Async XLA Ops:
  7.2 88.8 %all-gather.3.cloned.1.call-start = ((), (), s32[]{:S(2)}) async-start(), calls=%async_computation.7 | async-start | bytes 5013504 | tf_op jit(solution)/shard_map/all_gather | solution.py:108
  9.1 128.2 %reduce-scatter.5.cloned.1.call-start = ((), (), s32[]{:S(2)}) async-start(), calls=%async_computation.8 | async-start | bytes 7077888 | tf_op jit(solution)/shard_map/reduce_scatter | solution.py:25
  96.0 4.1 copy-start.4
  100.1 3.9 copy-start.5
  105.3 2.2 copy-start.6
  123.2 119.5 %copy-start.1 = (f32[2,3,192,128]{3,2,1,0:T(8,128)S(1)}, f32[2,3,192,128]{3,2,1,0:T(8,128)}, u32[]{:S(2)}) copy-start(f32[2,3,192,128]{3,2,1,0:T(8,128)} %param.16) | copy-start | bytes 1769476
  123.2 119.5 %copy-start.2 = (f32[2,3,192,128]{3,2,1,0:T(8,128)S(1)}, f32[2,3,192,128]{3,2,1,0:T(8,128)}, u32[]{:S(2)}) copy-start(f32[2,3,192,128]{3,2,1,0:T(8,128)} %param.17) | copy-start | bytes 1769476
  123.2 119.5 %copy-start.3 = (f32[2,3,192,128]{3,2,1,0:T(8,128)S(1)}, f32[2,3,192,128]{3,2,1,0:T(8,128)}, u32[]{:S(2)}) copy-start(f32[2,3,192,128]{3,2,1,0:T(8,128)} %param.18) | copy-start | bytes 1769476
  123.2 119.4 %reduce-scatter.7.cloned.1.call-start = ((), (), s32[]{:S(2)}) async-start(), calls=%async_computation.9 | async-start | bytes 2654208 | tf_op jit(solution)/shard_map/reduce_scatter | solution.py:26
  137.3 186.2 %all-gather.5.cloned.1.call-start = ((), (), s32[]{:S(2)}) async-start(), calls=%async_computation.10 | async-start | bytes 5013504 | tf_op jit(solution)/shard_map/all_gather | solution.py:162
  244.9 209.7 %reduce-scatter.9.cloned.1.call-start = ((), (), s32[]{:S(2)}) async-start(), calls=%async_computation.11 | async-start | bytes 10485760 | tf_op jit(solution)/shard_map/reduce_scatter | solution.py:32
  323.5 4.1 copy-start
  350.0 0.7 copy-start.7
  350.0 0.7 copy-start.8
  364.0 90.5 %all-to-all-start.2 = ((f32[4,2,3,192,128]{4,3,2,1,0:T(8,128)}), f32[4,2,3,192,128]{4,3,2,1,0:T(8,128)}, u32[]{:S(2)}, u32[]{:S(2)}) async-start(f32[4,2,3,192,128]{4,3,2,1,0:T(8,128)} %bitcast.99), calls=%async_computation.4 | async-start | bytes 4718592 | tf_op jit(solution)/shard_map/all_to_all | solution.py:148
  368.6 154.6 %reduce-scatter.11.cloned.1.call-start = ((), (), s32[]{:S(2)}) async-start(), calls=%async_computation.12 | async-start | bytes 2621440 | tf_op jit(solution)/shard_map/reduce_scatter | solution.py:32
  487.3 32.1 %all-to-all-start = ((f32[4,2,3,192,128]{4,3,2,1,0:T(8,128)}), f32[4,2,3,192,128]{4,3,2,1,0:T(8,128)S(1)}, u32[]{:S(2)}, u32[]{:S(2)}) async-start(f32[4,2,3,192,128]{4,3,2,1,0:T(8,128)} %bitcast.14), calls=%async_computation.2 | async-start | bytes 4718592 | tf_op jit(solution)/shard_map/all_to_all | solution.py:146
Sparse Core Ops, SparseCore 0:
  11.1 84.8 all-gather.2
  123.4 13.8 reduce-scatter.4
  142.0 100.6 reduce-scatter.6
  245.7 77.8 all-gather.4
  350.2 104.3 reduce-scatter.8
  456.9 48.0 reduce-scatter.10
where the time goes:
time: 532 us
  waiting for transfers between devices  393 us (74%)
  matrix products  48.1 us (9%)
  blocking collectives  32.7 us (6%)
  local copies, waits for them, and re-layouts  18.6 us (3%)
  other arithmetic  16.6 us (3%)
  between operations  14.4 us (3%)
  starting transfers between devices  8.42 us (2%)
    reduce_scatter x1, waiting for transfers between devices, summed_rows(): return lax.psum_scatter(pieces, chips, scatter_dimension=0, tiled=True)[0]  105 us
    reduce_scatter x2, waiting for transfers between devices, scatter_axes(): nearer = lax.psum_scatter(x, axes[0], scatter_dimension=dim, tiled=True)  85.9 us
    all_gather x1, waiting for transfers between devices, per_device(): full_weights = lax.all_gather(shard_weights, DP, axis=3, tiled=True)  85.3 us
    all_gather x1, waiting for transfers between devices, per_device(): next_full = lax.all_gather(next_shard, DP, axis=3, tiled=True)  78.6 us
    all_to_all x1, blocking collectives, per_device(): lax.all_to_all(outgoing(new_a), 'slot', split_axis=0, concat_axis=0, tile...  32.7 us
    all_to_all x1, waiting for transfers between devices, per_device(): lax.all_to_all(outgoing(new_master), 'slot', split_axis=0, concat_axis=0,...  23.8 us
    dot_general x8, matrix products, rows_by(): lax.dot_general(left, right, (((1,), (1,)), ((), ())), preferred_element_...  21.1 us
    dot_general x2, matrix products, expert_out(): return jnp.dot(mixed, weights[2], preferred_element_type=jnp.float32)  19.7 us
  transfers between devices with their start and end apart: 8, of which 6 were waited for; matrix products, arithmetic and copies ran while one was open for 4% of the time, Pallas kernels for 0%

commit v1 on v0

--- a/solution.py
+++ b/solution.py
@@ -105,7 +105,9 @@
     offset = slot_index * local_count
     held_ids = lax.dynamic_slice_in_dim(old_order, offset, local_count)
     shard_weights = master_weights.astype(jnp.bfloat16)
-    full_weights = lax.all_gather(shard_weights, DP, axis=3, tiled=True)
+    full_weights = jnp.concatenate(
+        lax.all_to_all(jnp.stack([shard_weights] * lax.axis_size(DP)), DP, 0, 0), axis=3
+    )
     scaling_one = coefficients(route_one, prob_one, held_ids)
     parts = [
         expert_parts(tokens_one, grad_out, scaling_one[:, expert], full_weights[expert])

time: 532 us -> 581 us (1.092)
  waiting for transfers between devices: 393 us -> 428 us
  starting transfers between devices: 8.42 us -> 20.2 us
  local copies, waits for them, and re-layouts: 18.6 us -> 27.1 us
    all_gather x1 -> x0, waiting for transfers between devices: 85.3 us -> none  [per_device(): full_weights = lax.all_gather(shard_weights, DP, axis=3, tiled=True)]
    all_to_all x0 -> x1, waiting for transfers between devices: none -> 66.4 us  [per_device(): lax.all_to_all(jnp.stack([shard_weights] * lax.axis_size(DP)), DP, 0, 0)]
    reduce_scatter x1, waiting for transfers between devices: 14 us -> 68.4 us  [summed_rows(): pieces = lax.psum_scatter(pieces, core, scatter_dimension=0, tiled=True)]
    all_to_all x0 -> x1, starting transfers between devices: none -> 11.6 us  [per_device(): lax.all_to_all(jnp.stack([shard_weights] * lax.axis_size(DP)), DP, 0, 0)]
    slice x0 -> x7, local copies, waits for them, and re-layouts: none -> 6.17 us  [the longest x3 4.12 us: expert_parts(): d_activated = rows_by(scaled_grad, weights[2])]
where the time goes in v1:
time: 581 us
  waiting for transfers between devices  428 us (74%)
  matrix products  43 us (7%)
  blocking collectives  32.7 us (6%)
  local copies, waits for them, and re-layouts  27.1 us (5%)
  starting transfers between devices  20.2 us (3%)
  other arithmetic  15.1 us (3%)
  between operations  14.1 us (2%)
    reduce_scatter x1, waiting for transfers between devices, summed_rows(): return lax.psum_scatter(pieces, chips, scatter_dimension=0, tiled=True)[0]  105 us
    reduce_scatter x2, waiting for transfers between devices, scatter_axes(): nearer = lax.psum_scatter(x, axes[0], scatter_dimension=dim, tiled=True)  85.9 us
    all_gather x1, waiting for transfers between devices, per_device(): next_full = lax.all_gather(next_shard, DP, axis=3, tiled=True)  78.5 us
    reduce_scatter x1, waiting for transfers between devices, summed_rows(): pieces = lax.psum_scatter(pieces, core, scatter_dimension=0, tiled=True)  68.4 us
    all_to_all x1, waiting for transfers between devices, per_device(): lax.all_to_all(jnp.stack([shard_weights] * lax.axis_size(DP)), DP, 0, 0)  66.4 us
    all_to_all x1, blocking collectives, per_device(): lax.all_to_all(outgoing(new_a), 'slot', split_axis=0, concat_axis=0, tile...  32.7 us
    all_to_all x1, waiting for transfers between devices, per_device(): lax.all_to_all(outgoing(new_master), 'slot', split_axis=0, concat_axis=0,...  23.8 us
    dot_general x2, matrix products, expert_out(): return jnp.dot(mixed, weights[2], preferred_element_type=jnp.float32)  19.7 us
  transfers between devices with their start and end apart: 8, of which 6 were waited for; matrix products, arithmetic and copies ran while one was open for 4% of the time, Pallas kernels for 0%

profile of v1, /device:TPU:2, one launch (start us, length us, event | category | flops | bytes accessed | tf_op | source)
XLA Modules:
  0.0 580.6 jit_solution(12360419744379263703)
XLA Ops:
  8.3 3.4 stack.20
  11.7 11.6 %all-to-all-start = ((bf16[16,2,3,192,128]{4,3,2,1,0:T(8,128)(2,1)}), bf16[16,2,3,192,128]{4,3,2,1,0:T(8,128)(2,1)}, u32[]{:S(2)}, u32[]{:S(2)}) async-start(bf16[16,2,3,192,128]{4,3,2,1,0:T(8,128)(2,1)} %stack.20), calls=%async_computation | async-start | bytes 9437184 | tf_op jit(solution)/shard_map/all_to_all | solution.py:109
  23.6 66.4 %all-to-all-done = bf16[16,2,3,192,128]{4,3,2,1,0:T(8,128)(2,1)} async-done(((bf16[16,2,3,192,128]{4,3,2,1,0:T(8,128)(2,1)}), bf16[16,2,3,192,128]{4,3,2,1,0:T(8,128)(2,1)}, u32[]{:S(2)}, u32[]{:S(2)}) %all-to-all-start) | async-done | bytes 4718624 | tf_op jit(solution)/shard_map/all_to_all | solution.py:109
  89.9 2.9 fusion.78
  114.4 3.4 copy.43
  117.9 68.4 %reduce-scatter.5.cloned.1.call-done = bf16[8,2,3,192,128]{4,3,2,1,0:T(8,128)(2,1)} async-done(((bf16[16,2,3,192,128]{4,3,2,1,0:T(8,128)(2,1)}), bf16[8,2,3,192,128]{4,3,2,1,0:T(8,128)(2,1)}) %reduce-scatter.5.cloned.1.call-update) | async-done | bytes 2359312 | tf_op jit(solution)/shard_map/reduce_scatter | solution.py:25
  186.4 105.3 %reduce-scatter.7.cloned.1.call-done = bf16[1,2,3,192,128]{4,3,2,1,0:T(8,128)(2,1)} async-done(((bf16[8,2,3,192,128]{4,3,2,1,0:T(8,128)(2,1)}), bf16[1,2,3,192,128]{4,3,2,1,0:T(8,128)(2,1)}) %reduce-scatter.7.cloned.1.call-update) | async-done | bytes 294928 | tf_op jit(solution)/shard_map/reduce_scatter | solution.py:26
  291.6 2.2 fusion.75
  294.1 78.5 %all-gather.2.cloned.1.call-done = bf16[2,3,192,2048]{3,2,1,0:T(8,128)(2,1)} async-done(((bf16[2,3,192,128]{3,2,1,0:T(8,128)(2,1)}), bf16[2,3,192,2048]{3,2,1,0:T(8,128)(2,1)}) %all-gather.2.cloned.1.call-update) | async-done | bytes 4718608 | tf_op jit(solution)/shard_map/all_gather | solution.py:164
  372.6 4.1 fusion.38
  376.8 2.7 fusion.37
  379.4 8.6 %fusion.19 = f32[1024,2048]{1,0:T(8,128)} fusion(bf16[1024,2048]{1,0:T(8,128)(2,1)} %param.23, bf16[2,3,192,2048]{3,2,1,0:T(8,128)(2,1)} %all-gather.2.cloned.1.call-done, f32[192,1024]{1,0:T(8,128)S(1)} %fusion.38, f32[1024]{0:T(1024)S(1)} %bitcast.128), kind=kOutput, calls=%fused_computation.29 | convolution fusion | flops 1611988992 | bytes 14946304 | tf_op jit(solution)/shard_map/dot_general | solution.py:69
  388.0 11.1 %convolution_add_fusion = f32[1024,2048]{1,0:T(8,128)} fusion(f32[1024,2048]{1,0:T(8,128)} %fusion.19, bf16[1024,2048]{1,0:T(8,128)(2,1)} %param.23, bf16[2,3,192,2048]{3,2,1,0:T(8,128)(2,1)} %all-gather.2.cloned.1.call-done, f32[192,1024]{1,0:T(8,128)S(1)} %fusion.37, f32[1024]{0:T(1024)S(1)} %bitcast.127), kind=kOutput, calls=%fused_computation.11 | convolution fusion | flops 1614086144 | bytes 23334912 | tf_op jit(solution)/shard_map/dot_general | solution.py:69
  402.1 2.2 gather_fusion.2
  404.3 2.2 gather_fusion
  406.5 6.7 %broadcast_select_fusion = (f32[8,3,192,128]{3,2,1,0:T(8,128)}, f32[8,3,192,128]{3,2,1,0:T(8,128)S(1)}, f32[8,3,192,128]{3,2,1,0:T(8,128)}) fusion(f32[8,3,192,128]{3,2,1,0:T(8,128)} %gather_fusion.4, pred[8]{0:T(512)(128)(4,1)S(1)} %get-tuple-element.14, f32[8,3,192,128]{3,2,1,0:T(8,128)} %gather_fusion.2, f32[8,3,192,128]{3,2,1,0:T(8,128)} %gather_fusion), kind=kLoop, calls=%fused_computation.31 | loop fusion | flops 1769472 | bytes 14155784 | tf_op jit(solution)/shard_map/jit(_take)/select_n | solution.py:144
  413.1 4.6 all-to-all-start.3
  417.8 85.9 %reduce-scatter.9.cloned.1.call-done = f32[1024,512]{1,0:T(8,128)} async-done(((f32[1024,2048]{1,0:T(8,128)}), f32[1024,512]{1,0:T(8,128)}) %reduce-scatter.9.cloned.1.call-update) | async-done | bytes 2097168 | tf_op jit(solution)/shard_map/reduce_scatter | solution.py:32
  503.7 32.7 %all_to_all.20 = f32[4,2,3,192,128]{4,3,2,1,0:T(8,128)} all-to-all(f32[4,2,3,192,128]{4,3,2,1,0:T(8,128)S(1)} %bitcast.111), channel_id=1, replica_groups=mesh['dp_0'=2,'dp_1'=4,'dp_2'=2,'slot'=4,'hid'=4] {'slot'}, dimensions={0} | all-to-all | bytes 4718592 | tf_op jit(solution)/shard_map/all_to_all | solution.py:149
  536.4 3.6 all-to-all-start.1
  540.2 2.2 gather_fusion.5
  542.4 2.2 gather_fusion.3
  544.7 23.8 %all-to-all-done.1 = f32[4,2,3,192,128]{4,3,2,1,0:T(8,128)S(1)} async-done(((f32[4,2,3,192,128]{4,3,2,1,0:T(8,128)}), f32[4,2,3,192,128]{4,3,2,1,0:T(8,128)S(1)}, u32[]{:S(2)}, u32[]{:S(2)}) %all-to-all-start.1) | async-done | bytes 2359328 | tf_op jit(solution)/shard_map/all_to_all | solution.py:148
  569.9 2.4 broadcast_select_fusion.3
  (74 shorter events, 29.4 us)
Async XLA Ops:
  11.6 11.7 %copy-start.10 = (s32[8]{0:T(128)S(1)}, s32[8]{0:T(128)}, u32[]{:S(2)}) copy-start(s32[8]{0:T(128)} %param.26) | copy-start | bytes 100
  11.6 11.8 %copy-start.4 = (f32[1024,2]{0,1:T(2,128)S(1)}, f32[1024,2]{0,1:T(2,128)}, u32[]{:S(2)}) copy-start(f32[1024,2]{0,1:T(2,128)} %param.25) | copy-start | bytes 24580
  11.7 11.8 %copy-start.5 = (s32[1024,2]{0,1:T(2,128)S(1)}, s32[1024,2]{0,1:T(2,128)}, u32[]{:S(2)}) copy-start(s32[1024,2]{0,1:T(2,128)} %param.24) | copy-start | bytes 24580
  11.7 11.8 %copy-start.6 = (f32[1024,2]{0,1:T(2,128)S(1)}, f32[1024,2]{0,1:T(2,128)}, u32[]{:S(2)}) copy-start(f32[1024,2]{0,1:T(2,128)} %param.22) | copy-start | bytes 24580
  11.7 11.8 %copy-start.7 = (s32[1024,2]{0,1:T(2,128)S(1)}, s32[1024,2]{0,1:T(2,128)}, u32[]{:S(2)}) copy-start(s32[1024,2]{0,1:T(2,128)} %param.21) | copy-start | bytes 24580
  11.7 78.2 %all-to-all-start = ((bf16[16,2,3,192,128]{4,3,2,1,0:T(8,128)(2,1)}), bf16[16,2,3,192,128]{4,3,2,1,0:T(8,128)(2,1)}, u32[]{:S(2)}, u32[]{:S(2)}) async-start(bf16[16,2,3,192,128]{4,3,2,1,0:T(8,128)(2,1)} %stack.20), calls=%async_computation | async-start | bytes 9437184 | tf_op jit(solution)/shard_map/all_to_all | solution.py:109
  23.3 163.0 %reduce-scatter.5.cloned.1.call-start = ((), (), s32[]{:S(2)}) async-start(), calls=%async_computation.8 | async-start | bytes 7077888 | tf_op jit(solution)/shard_map/reduce_scatter | solution.py:25
  89.9 4.0 copy-start.9
  95.4 2.2 copy-start.8
  117.8 173.8 %copy-start.1 = (f32[2,3,192,128]{3,2,1,0:T(8,128)S(1)}, f32[2,3,192,128]{3,2,1,0:T(8,128)}, u32[]{:S(2)}) copy-start(f32[2,3,192,128]{3,2,1,0:T(8,128)} %param.16) | copy-start | bytes 1769476
  117.8 173.9 %copy-start.2 = (f32[2,3,192,128]{3,2,1,0:T(8,128)S(1)}, f32[2,3,192,128]{3,2,1,0:T(8,128)}, u32[]{:S(2)}) copy-start(f32[2,3,192,128]{3,2,1,0:T(8,128)} %param.17) | copy-start | bytes 1769476
  117.8 173.9 %copy-start.3 = (f32[2,3,192,128]{3,2,1,0:T(8,128)S(1)}, f32[2,3,192,128]{3,2,1,0:T(8,128)}, u32[]{:S(2)}) copy-start(f32[2,3,192,128]{3,2,1,0:T(8,128)} %param.18) | copy-start | bytes 1769476
  117.8 173.8 %reduce-scatter.7.cloned.1.call-start = ((), (), s32[]{:S(2)}) async-start(), calls=%async_computation.9 | async-start | bytes 2654208 | tf_op jit(solution)/shard_map/reduce_scatter | solution.py:26
  186.3 186.3 %all-gather.2.cloned.1.call-start = ((), (), s32[]{:S(2)}) async-start(), calls=%async_computation.10 | async-start | bytes 5013504 | tf_op jit(solution)/shard_map/all_gather | solution.py:164
  293.8 209.8 %reduce-scatter.9.cloned.1.call-start = ((), (), s32[]{:S(2)}) async-start(), calls=%async_computation.11 | async-start | bytes 10485760 | tf_op jit(solution)/shard_map/reduce_scatter | solution.py:32
  372.6 4.1 copy-start
  399.1 0.7 copy-start.11
  413.1 90.5 %all-to-all-start.3 = ((f32[4,2,3,192,128]{4,3,2,1,0:T(8,128)}), f32[4,2,3,192,128]{4,3,2,1,0:T(8,128)}, u32[]{:S(2)}, u32[]{:S(2)}) async-start(f32[4,2,3,192,128]{4,3,2,1,0:T(8,128)} %bitcast.112), calls=%async_computation.5 | async-start | bytes 4718592 | tf_op jit(solution)/shard_map/all_to_all | solution.py:150
  417.7 154.5 %reduce-scatter.11.cloned.1.call-start = ((), (), s32[]{:S(2)}) async-start(), calls=%async_computation.12 | async-start | bytes 2621440 | tf_op jit(solution)/shard_map/reduce_scatter | solution.py:32
  536.4 32.1 %all-to-all-start.1 = ((f32[4,2,3,192,128]{4,3,2,1,0:T(8,128)}), f32[4,2,3,192,128]{4,3,2,1,0:T(8,128)S(1)}, u32[]{:S(2)}, u32[]{:S(2)}) async-start(f32[4,2,3,192,128]{4,3,2,1,0:T(8,128)} %bitcast.9), calls=%async_computation.3 | async-start | bytes 4718592 | tf_op jit(solution)/shard_map/all_to_all | solution.py:148
Sparse Core Ops, SparseCore 0:
  117.9 68.3 reduce-scatter.4
  191.0 100.6 reduce-scatter.6
  294.8 77.8 all-gather.1
  399.3 104.3 reduce-scatter.8
  506.0 48.0 reduce-scatter.10
